TPU v7x, 32 devices: a whole 2x2x4 slice. The times are simulated.
32 devices in a mesh: district: 2 (over x), tiles: 16 (over z, y, core).
Axes of the slice: x: 2, y: 2, z: 4, core: 2. Of those that a mesh axis runs over, the one named last changes fastest.
Arguments:
- sky: bfloat16 [336, 2306], P('district'), parts along dimension 0, may hold values from -6 to 6
- coeffs: bfloat16 [2306, 32768], P(None, ('district', 'tiles')), parts along dimension 1, may hold values from -0.125 to 0.125
- albedo: float32 [32768], P(('district', 'tiles')), parts along dimension 0, may hold values from 0.1 to 0.9
- view_blocks: bfloat16 [2048, 128, 128], P(('district', 'tiles')), parts along dimension 0, may hold values from -0.1875 to 0.1875
- block_rows: int32 [2048], P(('district', 'tiles')), parts along dimension 0, may hold values from 0 to 127, as said below
- block_cols: int32 [2048], P(('district', 'tiles')), parts along dimension 0, may hold values from 0 to 127, as said below
- counts: int32 [32], P(('district', 'tiles')), parts along dimension 0, may hold values from 8 to 64, as said below
Outputs:
- irradiance: float32 [168, 32768], P(None, ('district', 'tiles')), parts along dimension 1
There are 2 independent parts, one for each index of `district`. A program takes and returns all parts, laid end to end along the dimension named above; each array names one. Nothing has to cross between parts.
Inputs may be any that keep to these rules, and one draw needn't show every extreme that they name: `block_rows`: slots of group g (slots g * 64 to (g + 1) * 64 - 1) name receiving blocks of group g's own tiles, that is g * 8 to (g + 1) * 8 - 1. `block_cols`: the slots of one group name at most 2 distinct sending blocks among the tiles of any one group, and exactly 2 among those of some group. Slots of group g at positions counts[g] and beyond are unused; some group has all 64 slots live.
All inputs are finite; a program needn't handle non-finite values.
Results may differ from a plain program's by a relative error of at most 0.0011.
Values may be sent and summed in bfloat16 or wider, within the bound.
No kernel may reach another device: no remote copies, remote signals or barrier semaphores. Data moves between devices by JAX's collectives and lax.ppermute only.
A program may use at most 128 MiB of HBM per device.

v0:
```python
import functools

import jax
import jax.numpy as jnp
from jax import lax
from jax.experimental import pallas as pl
from jax.experimental.pallas import tpu as pltpu
from jax.sharding import PartitionSpec as P

NEAR = 8
AT_ONCE = 8
SMEM = pl.BlockSpec(memory_space=pltpu.SMEM)
VMEM = pl.BlockSpec(memory_space=pltpu.VMEM)
ANY = pl.BlockSpec(memory_space=pl.ANY)
HBM = pl.BlockSpec(memory_space=pltpu.HBM)


def product_kernel(cuts, after_ref, sky_ref, coeffs_ref, albedo_ref, out_ref, last_ref, sky, *scratch):
    del after_ref
    *coeffs, total, sems = scratch
    whole_sky = pltpu.make_async_copy(sky_ref, sky, sems.at[len(coeffs)])
    copies = [
        pltpu.make_async_copy(coeffs_ref.at[pl.ds(start, stop - start)], part, sems.at[number])
        for number, (start, stop, part) in enumerate(zip(cuts, cuts[1:], coeffs))
    ]
    copies[0].start()
    whole_sky.start()
    for copy in copies[1:]:
        copy.start()
    last_ref[...] = jnp.zeros_like(last_ref)
    whole_sky.wait()
    for copy, start, stop, part in zip(copies, cuts, cuts[1:], coeffs):
        copy.wait()
        direct = jnp.dot(sky[:, start:stop], part[...], preferred_element_type=jnp.float32)
        if start:
            direct += total[...]
        if stop < cuts[-1]:
            total[...] = direct
    if len(out_ref.shape) == 2:
        out_ref[...] = direct
        return
    emitted = (albedo_ref[...] * direct).astype(jnp.bfloat16)
    block = out_ref.shape[2]
    for k in range(out_ref.shape[0]):
        out_ref[k] = emitted[:, k * block : (k + 1) * block]


def product(after, sky, coeffs, albedo, out, depth, name):
    patches, tiles = coeffs.shape
    cuts = [*range(0, patches - depth + 1, depth), patches]
    return pl.pallas_call(
        functools.partial(product_kernel, cuts),
        in_specs=[ANY, HBM, HBM, VMEM],
        out_specs=[VMEM, VMEM],
        out_shape=[out, jax.ShapeDtypeStruct((1, 128), jnp.int32)],
        scratch_shapes=[
            pltpu.VMEM(sky.shape, sky.dtype),
            *[pltpu.VMEM((stop - start, tiles), coeffs.dtype) for start, stop in zip(cuts, cuts[1:])],
            pltpu.VMEM((sky.shape[0], tiles), jnp.float32),
            pltpu.SemaphoreType.DMA((len(cuts),)),
        ],
        compiler_params=pltpu.CompilerParams(vmem_limit_bytes=62 * 2**20),
        name=name,
    )(after, sky, coeffs, albedo)


def reads_kernel(blocks, groups, cols_ref, reads_ref):
    slots, width = cols_ref.shape[1], reads_ref.shape[1]
    group = lax.broadcasted_iota(jnp.int32, (groups, slots), 0)
    inside = jnp.broadcast_to(cols_ref[...], (groups, slots)) - group * blocks
    read = (inside >= 0) & (inside < blocks)
    lo = jnp.min(jnp.where(read, inside, blocks - 1), axis=1, keepdims=True)
    hi = jnp.max(jnp.where(read, inside, 0), axis=1, keepdims=True)
    group = lax.broadcasted_iota(jnp.int32, (groups, width), 0)
    lane = lax.broadcasted_iota(jnp.int32, (groups, width), 1)
    row = jnp.where(lane == group, lo, 0) + jnp.where(lane == group + groups, hi, 0)
    live = jnp.sum((cols_ref[...] >= 0).astype(jnp.int32), axis=1, keepdims=True)
    reads_ref[...] = jnp.sum(row, axis=0, keepdims=True) + jnp.where(lane[0:1] == 2 * groups, live, 0)


def blocks_read(cols, blocks, groups):
    width = -(-(2 * groups + 1) // 128) * 128
    return pl.pallas_call(
        functools.partial(reads_kernel, blocks, groups),
        in_specs=[VMEM],
        out_specs=VMEM,
        out_shape=jax.ShapeDtypeStruct((1, width), jnp.int32),
        compiler_params=pltpu.CompilerParams(vmem_limit_bytes=2**20),
        name="reads",
    )(cols.reshape(1, -1))


def pack_kernel(wanted, groups, me_ref, table_ref, *refs):
    held, outs = refs[: -len(wanted)], refs[-len(wanted) :]
    for out, (peer, sends) in zip(outs, wanted):
        for at, (which, bits, end) in enumerate(sends):
            out[at] = held[which][table_ref[peer, (me_ref[0] ^ bits) + groups * end]]


def pack(me, table, groups, held, wanted):
    return pl.pallas_call(
        functools.partial(pack_kernel, wanted, groups),
        in_specs=[SMEM, SMEM] + [VMEM] * len(held),
        out_specs=[VMEM] * len(wanted),
        out_shape=[pltpu.VMEM((len(sends),) + held[0].shape[1:], held[0].dtype) for _, sends in wanted],
        compiler_params=pltpu.CompilerParams(vmem_limit_bytes=24 * 2**20),
        name="pack",
    )(me, table, *held)


def plan_kernel(blocks, rooms, groups, me_ref, rows_ref, cols_ref, reads_ref, phase_ref, base_ref, local_ref, *refs):
    order_ref = refs[-1]
    phases, places = order_ref.shape

    def clear(i, carry):
        for at in range(phases):
            order_ref[at, i] = rooms[at] * 4096
        return carry

    lax.fori_loop(1, places, clear, 0)
    for at in range(phases):
        order_ref[at, 0] = 0

    def step(slot, carry):
        col = cols_ref[slot]
        group = col // blocks
        kind = group ^ me_ref[0]
        inside = col - group * blocks
        local = local_ref[kind] == 1
        end = (inside == reads_ref[0, groups + group]).astype(jnp.int32)
        source = base_ref[kind] + jnp.where(local, inside, end)
        row = rows_ref[slot] - me_ref[0] * blocks
        phase = phase_ref[kind]
        at = order_ref[phase, 0] + 1
        order_ref[phase, at] = slot + row * 256 + source * 4096
        order_ref[phase, 0] = at
        return carry

    lax.fori_loop(0, reads_ref[0, 2 * groups], step, 0)


def plan(me, rows, cols, reads, phase, base, local, after, blocks, rooms):
    return pl.pallas_call(
        functools.partial(plan_kernel, blocks, rooms, phase.shape[0]),
        in_specs=[SMEM] * 7 + [ANY] * len(after),
        out_specs=SMEM,
        out_shape=jax.ShapeDtypeStruct((len(rooms), 1 + rows.shape[0] + AT_ONCE), jnp.int32),
        compiler_params=pltpu.CompilerParams(vmem_limit_bytes=2**20),
        name="plan",
    )(me, rows, cols, reads, phase, base, local, *after)


def reflect_kernel(phase, order_ref, total_ref, views_ref, *refs):
    sources, (out_ref, pool, order, sems) = refs[:-4], refs[-4:]
    copies = [pltpu.make_async_copy(order_ref, order, sems.at[len(sources) + 1])]
    if phase == 0:
        copies.append(pltpu.make_async_copy(total_ref, out_ref, sems.at[len(sources)]))
    room = 0
    for number, source in enumerate(sources):
        length = source.shape[0]
        if phase < 2:
            copies.append(pltpu.make_async_copy(source, pool.at[pl.ds(room, length)], sems.at[number]))
        else:
            pool[room : room + length] = source[...]
        room += length
    for copy in copies:
        copy.start()
    pool[room] = jnp.zeros(pool.shape[1:], pool.dtype)
    if phase:
        out_ref[...] = total_ref[...]
    for copy in copies:
        copy.wait()
    block = views_ref.shape[1]

    def step(i, carry):
        entries = [order[phase, 1 + i * AT_ONCE + k] for k in range(AT_ONCE)]
        parts = [
            lax.dot_general(
                pool[entry // 4096],
                views_ref[entry & 255],
                (((1,), (1,)), ((), ())),
                preferred_element_type=jnp.float32,
            )
            for entry in entries
        ]
        for entry, part in zip(entries, parts):
            columns = pl.ds(pl.multiple_of(((entry // 256) & 15) * block, block), block)
            out_ref[:, columns] += part
        return carry

    lax.fori_loop(0, (order[phase, 0] + AT_ONCE - 1) // AT_ONCE, step, 0)


def reflect(phase, order, total, view_blocks, sources):
    room = sum(source.shape[0] for source in sources)
    return pl.pallas_call(
        functools.partial(reflect_kernel, phase),
        in_specs=[HBM, HBM if phase == 0 else VMEM, VMEM] + [ANY if phase < 2 else VMEM] * len(sources),
        out_specs=VMEM,
        out_shape=jax.ShapeDtypeStruct(total.shape, total.dtype),
        scratch_shapes=[
            pltpu.VMEM((room + 1,) + sources[0].shape[1:], sources[0].dtype),
            pltpu.SMEM(order.shape, order.dtype),
            pltpu.SemaphoreType.DMA((len(sources) + 2,)),
        ],
        compiler_params=pltpu.CompilerParams(vmem_limit_bytes=24 * 2**20),
        name="reflect",
    )(order, total, view_blocks, *sources)


def per_device(sky, coeffs, albedo, view_blocks, block_rows, block_cols, counts):
    peers = lax.axis_size("tiles")
    me = lax.axis_index("tiles").astype(jnp.int32).reshape(1)
    block = view_blocks.shape[1]
    blocks = coeffs.shape[1] // block
    rest = peers // NEAR - 1
    far = [NEAR * k for k in range(1, rest + 1)]
    core, beside, below = 1, 2, 4

    def swap(x, bits):
        return lax.ppermute(x, "tiles", [(i, i ^ bits) for i in range(peers)])

    hours, tiles = sky.shape[0], coeffs.shape[1]
    albedo = albedo.reshape(1, -1)
    emitted, zeros = product(
        me, sky, coeffs, albedo, pltpu.VMEM((blocks, hours, block), jnp.bfloat16), 2 * block, "emitted"
    )

    far_held = [swap(emitted, bits) for bits in far]
    below_held = swap(emitted, below)
    beside_held = swap(emitted, beside)

    live = jnp.arange(block_cols.shape[0], dtype=jnp.int32) < counts[0] + zeros[0, 0]
    reads = blocks_read(jnp.where(live, block_cols, -1), blocks, peers)
    table = jnp.concatenate([reads, swap(reads, beside)])
    below_table = swap(table, below)
    direct, zeros = product(
        reads, sky, coeffs, albedo, jax.ShapeDtypeStruct((hours, tiles), jnp.float32), 2 * block, "direct"
    )

    place = {kind: (0, blocks * kind) for kind in range(below)}
    place[below] = (1, 2 * blocks * rest)
    place[below + core] = (1, 2 * blocks * rest + blocks)
    place[below + beside + core] = (1, 2 * blocks * (rest + 1) + 4 * rest)
    place[below + beside] = (2, 4 * rest)
    local = {*range(below), below, below + core}
    for h, bits in enumerate(far):
        for c in range(2):
            local.add(bits + c)
            place[bits + c] = (1, blocks * (2 * h + c))
            place[bits + beside + c] = (1, 2 * blocks * (rest + 1) + 4 * h + 2 * c)
            place[bits + below + c] = (2, 4 * h + 2 * c)
            place[bits + below + beside + c] = (2, 4 * rest + 2 + 4 * h + 2 * c)
    rooms = [4 * blocks, 2 * blocks * (rest + 1) + 4 * rest + 2, 8 * rest + 2]
    order = plan(
        me,
        block_rows,
        block_cols,
        reads,
        jnp.array([place[kind][0] for kind in range(peers)], jnp.int32),
        jnp.array([place[kind][1] for kind in range(peers)], jnp.int32),
        jnp.array([int(kind in local) for kind in range(peers)], jnp.int32),
        [zeros],
        blocks,
        rooms,
    )
    order, below_table, below_held, far_held = lax.optimization_barrier((order, below_table, below_held, far_held))
    table = jnp.concatenate([table, below_table])
    held = [x for shard in far_held for x in (shard, swap(shard, core))]
    below_pair = [below_held, swap(below_held, core)]
    near = [emitted, swap(emitted, core), beside_held, swap(beside_held, core)]

    wanted = [(2 * h + c, far[h] + c, end) for h in range(rest) for c in range(2) for end in range(2)]
    from_beside = [(2 * rest, below + core, end) for end in range(2)]
    from_below = [(2 * rest + 1, beside, end) for end in range(2)]
    sends = [(1, wanted + from_beside), (2, wanted + from_below), (3, wanted)]
    others = pack(me, table, peers, held + [below_pair[1], beside_held], sends)
    late = [swap(x, bits) for x, bits in zip(others, (beside, below, below + beside))]

    direct, _ = lax.optimization_barrier((direct, others[0]))
    total = reflect(0, order, direct, view_blocks, near)
    total = reflect(1, order, total, view_blocks, held + below_pair + late[:1])
    return reflect(2, order, total, view_blocks, late[1:])


def solution(mesh):
    in_specs = (
        P("district", None),
        P(None, ("district", "tiles")),
        P(("district", "tiles")),
        P(("district", "tiles"), None, None),
        P(("district", "tiles")),
        P(("district", "tiles")),
        P(("district", "tiles")),
    )
    out_specs = P(None, ("district", "tiles"))
    return jax.shard_map(
        per_device, mesh=mesh, in_specs=in_specs, out_specs=out_specs, check_vma=False
    )
```

profile of v0, /device:TPU:0, one launch (start us, length us, event | category | flops | bytes accessed | tf_op | source)
XLA Modules:
  0.0 42.5 jit_solution(463819886790068020)
XLA Ops:
  0.0 0.0 copy-start.6
  0.0 0.0 copy-start.5
  0.0 0.0 copy-start.7
  0.0 0.0 copy-start.8
  0.0 0.0 copy-start.9
  0.0 3.9 %emitted.1 = (bf16[8,168,128]{2,1,0:T(8,128)(2,1)S(1)}, s32[1,128]{1,0:T(1,128)}) custom-call(s32[1]{0:T(128)} %bitcast.after_ref.me_ref, bf16[168,2306]{1,0:T(8,128)(2,1)} %sky_ref.3, bf16[2306,1024]{1,0:T(8,128)(2,1)} %coeffs_ref.3, f32[1,1024]{1,0:T(1,128)} %bitcast.8), custom_call_target="tpu_custom_call" | custom-call | tf_op jit(solution)/shard_map/emitted/pallas_call | solution.py:51
  3.9 4.1 %collective-permute-start.3 = (bf16[8,168,128]{2,1,0:T(8,128)(2,1)S(1)}, bf16[8,168,128]{2,1,0:T(8,128)(2,1)S(1)}, u32[]{:S(2)}, u32[]{:S(2)}) collective-permute-start(bf16[8,168,128]{2,1,0:T(8,128)(2,1)S(1)} %get-tuple-element.19.refs_0_), channel_id=1, source_target_pairs={{0,8},{1,9},{2,10},{3,11},{4,12},{5,13},{6,14},{7,15},{8,0},{9,1},... | collective-permute-start | bytes 1032200 | tf_op jit(solution)/shard_map/ppermute | solution.py:221
  8.0 1.6 %collective-permute-start.2 = (bf16[8,168,128]{2,1,0:T(8,128)(2,1)S(1)}, bf16[8,168,128]{2,1,0:T(8,128)(2,1)S(1)}, u32[]{:S(2)}, u32[]{:S(2)}) collective-permute-start(bf16[8,168,128]{2,1,0:T(8,128)(2,1)S(1)} %get-tuple-element.19.refs_0_), channel_id=1, source_target_pairs={{0,4},{1,5},{2,6},{3,7},{4,0},{5,1},{6,2},{7,3},{8,12},{9,13},{10,... | collective-permute-start | bytes 1032200 | tf_op jit(solution)/shard_map/ppermute | solution.py:221
  10.8 0.0 copy-done.6
  10.8 0.2 reads.1.after_ref.reads_ref
  11.0 0.0 copy-start.3
  11.0 1.6 %collective-permute-start = (s32[1,128]{1,0:T(1,128)S(1)}, s32[1,128]{1,0:T(1,128)S(1)}, u32[]{:S(2)}, u32[]{:S(2)}) collective-permute-start(s32[1,128]{1,0:T(1,128)S(1)} %reads.1.after_ref.reads_ref), channel_id=1, source_target_pairs={{0,2},{1,3},{2,0},{3,1},{4,6},{5,7},{6,4},{7,5},{8,10},{9,11},{10,... | collective-permute-start | bytes 1544 | tf_op jit(solution)/shard_map/ppermute | solution.py:221
  12.6 0.5 %collective-permute-start.6 = (bf16[8,168,128]{2,1,0:T(8,128)(2,1)S(1)}, bf16[8,168,128]{2,1,0:T(8,128)(2,1)S(1)}, u32[]{:S(2)}, u32[]{:S(2)}) collective-permute-start(bf16[8,168,128]{2,1,0:T(8,128)(2,1)S(1)} %get-tuple-element.19.refs_0_), channel_id=1, source_target_pairs={{0,2},{1,3},{2,0},{3,1},{4,6},{5,7},{6,4},{7,5},{8,10},{9,11},{10,... | collective-permute-start | bytes 1032200 | tf_op jit(solution)/shard_map/ppermute | solution.py:221
  13.1 1.5 %collective-permute-done = s32[1,128]{1,0:T(1,128)S(1)} collective-permute-done((s32[1,128]{1,0:T(1,128)S(1)}, s32[1,128]{1,0:T(1,128)S(1)}, u32[]{:S(2)}, u32[]{:S(2)}) %collective-permute-start) | collective-permute-done | bytes 544 | tf_op jit(solution)/shard_map/ppermute | solution.py:221
  14.7 0.4 %collective-permute-start.1 = (s32[2,128]{1,0:T(2,128)S(1)}, s32[2,128]{1,0:T(2,128)S(1)}, u32[]{:S(2)}, u32[]{:S(2)}) collective-permute-start(s32[2,128]{1,0:T(2,128)S(1)} %pad_add_fusion.1), channel_id=1, source_target_pairs={{0,4},{1,5},{2,6},{3,7},{4,0},{5,1},{6,2},{7,3},{8,12},{9,13},{10,... | collective-permute-start | bytes 3080 | tf_op jit(solution)/shard_map/ppermute | solution.py:221
  15.1 0.0 copy-done.3
  15.1 4.5 %direct.1 = (f32[168,1024]{1,0:T(8,128)}, s32[1,128]{1,0:T(1,128)}) custom-call(s32[1,128]{1,0:T(1,128)} %copy-done.3, bf16[168,2306]{1,0:T(8,128)(2,1)} %sky_ref.3, bf16[2306,1024]{1,0:T(8,128)(2,1)} %coeffs_ref.3, f32[1,1024]{1,0:T(1,128)} %bitcast.9), custom_call_target="tpu_custom_call" | custom-call | tf_op jit(solution)/shard_map/direct/pallas_call | solution.py:51
  19.6 0.0 copy-done.5
  19.6 0.0 copy-done.7
  19.7 0.0 copy-done.8
  19.7 0.0 copy-done.9
  19.7 0.0 copy-start.4
  19.7 0.6 %copy-done.4 = s32[1,128]{1,0:T(1,128)S(1)} copy-done((s32[1,128]{1,0:T(1,128)S(1)}, s32[1,128]{1,0:T(1,128)}, u32[]{:S(2)}) %copy-start.4) | copy-done | bytes 536
  20.3 0.0 copy-start.10
  20.3 0.7 %copy-done.10 = s32[1,128]{1,0:T(1,128)S(1)} copy-done((s32[1,128]{1,0:T(1,128)S(1)}, s32[1,128]{1,0:T(1,128)}, u32[]{:S(2)}) %copy-start.10) | copy-done | bytes 536
  20.9 3.3 %plan.1.order_ref = s32[3,73]{1,0:T(4,128)S(1)} custom-call(s32[1]{0:T(128)} %bitcast.after_ref.me_ref, s32[64]{0:T(128)S(1)} %copy-done.5, s32[64]{0:T(128)S(1)} %copy-done.6, s32[1,128]{1,0:T(1,128)S(1)} %copy-done.4, s32[16]{0:T(128)S(1)} %copy-done.9, s32[16]{0:T(128)S(1)} %copy-done.8, s32[16]{0:T(128)S(1)} %copy-done.7, s32[1,128]{1,0:T(1,128)S(1)} %copy-done.10), custom_call_target="tpu_custom_call" | custom-call | tf_op jit(solution)/shard_map/plan/pallas_call | solution.py:143
  24.2 0.0 collective-permute-done.1
  24.3 0.0 collective-permute-done.3.refs_0_
  24.3 0.0 collective-permute-done.2.refs_2_
  24.3 0.1 collective-permute-start.5
  24.4 0.5 %collective-permute-start.4 = (bf16[8,168,128]{2,1,0:T(8,128)(2,1)S(1)}, bf16[8,168,128]{2,1,0:T(8,128)(2,1)S(1)}, u32[]{:S(2)}, u32[]{:S(2)}) collective-permute-start(bf16[8,168,128]{2,1,0:T(8,128)(2,1)S(1)} %collective-permute-done.3.refs_0_), channel_id=1, source_target_pairs={{0,1},{1,0},{2,3},{3,2},{4,5},{5,4},{6,7},{7,6},{8,9},{9,8},{10,11... | collective-permute-start | bytes 1032200 | tf_op jit(solution)/shard_map/ppermute | solution.py:221
  24.9 0.1 collective-permute-start.7
  24.9 0.0 collective-permute-done.6.refs_3_.refs_2_
  24.9 0.4 %collective-permute-start.8 = (bf16[8,168,128]{2,1,0:T(8,128)(2,1)S(1)}, bf16[8,168,128]{2,1,0:T(8,128)(2,1)S(1)}, u32[]{:S(2)}, u32[]{:S(2)}) collective-permute-start(bf16[8,168,128]{2,1,0:T(8,128)(2,1)S(1)} %collective-permute-done.6.refs_3_.refs_2_), channel_id=1, source_target_pairs={{0,1},{1,0},{2,3},{3,2},{4,5},{5,4},{6,7},{7,6},{8,9},{9,8},{10,11... | collective-permute-start | bytes 1032200 | tf_op jit(solution)/shard_map/ppermute | solution.py:221
  25.4 0.6 %pad_add_fusion.table_ref = s32[4,128]{1,0:T(4,128)S(1)} fusion(s32[2,128]{1,0:T(2,128)S(1)} %collective-permute-done.1, s32[1,128]{1,0:T(1,128)S(1)} %collective-permute-done, s32[1,128]{1,0:T(1,128)} %copy-done.3), kind=kLoop, calls=%fused_computation | loop fusion | flops 1024 | bytes 4096 | tf_op jit(solution)/shard_map/concatenate | solution.py:268
  26.0 0.0 collective-permute-done.5.refs_2_.refs_3_
  26.0 0.5 %collective-permute-done.4.refs_1_ = bf16[8,168,128]{2,1,0:T(8,128)(2,1)S(1)} collective-permute-done((bf16[8,168,128]{2,1,0:T(8,128)(2,1)S(1)}, bf16[8,168,128]{2,1,0:T(8,128)(2,1)S(1)}, u32[]{:S(2)}, u32[]{:S(2)}) %collective-permute-start.4) | collective-permute-done | bytes 344096 | tf_op jit(solution)/shard_map/ppermute | solution.py:221
  26.5 0.6 %pack.1 = (bf16[6,168,128]{2,1,0:T(8,128)(2,1)S(1)}, bf16[6,168,128]{2,1,0:T(8,128)(2,1)S(1)}, bf16[4,168,128]{2,1,0:T(8,128)(2,1)S(1)}) custom-call(s32[1]{0:T(128)} %bitcast.after_ref.me_ref, s32[4,128]{1,0:T(4,128)S(1)} %pad_add_fusion.table_ref, bf16[8,168,128]{2,1,0:T(8,128)(2,1)S(1)} %collective-permute-done.3.refs_0_, ...), custom_call_target="tpu_custom_call" | custom-call | tf_op jit(solution)/shard_map/pack/pallas_call | solution.py:101
  27.1 1.1 %collective-permute-start.9 = (bf16[6,168,128]{2,1,0:T(8,128)(2,1)S(1)}, bf16[6,168,128]{2,1,0:T(8,128)(2,1)S(1)}, u32[]{:S(2)}, u32[]{:S(2)}) collective-permute-start(bf16[6,168,128]{2,1,0:T(8,128)(2,1)S(1)} %get-tuple-element.25), channel_id=1, source_target_pairs={{0,2},{1,3},{2,0},{3,1},{4,6},{5,7},{6,4},{7,5},{8,10},{9,11},{10,... | collective-permute-start | bytes 774152 | tf_op jit(solution)/shard_map/ppermute | solution.py:221
  28.2 1.4 %collective-permute-start.10 = (bf16[6,168,128]{2,1,0:T(8,128)(2,1)S(1)}, bf16[6,168,128]{2,1,0:T(8,128)(2,1)S(1)}, u32[]{:S(2)}, u32[]{:S(2)}) collective-permute-start(bf16[6,168,128]{2,1,0:T(8,128)(2,1)S(1)} %get-tuple-element.27), channel_id=1, source_target_pairs={{0,4},{1,5},{2,6},{3,7},{4,0},{5,1},{6,2},{7,3},{8,12},{9,13},{10,... | collective-permute-start | bytes 774152 | tf_op jit(solution)/shard_map/ppermute | solution.py:221
  29.7 1.0 %collective-permute-start.11 = (bf16[4,168,128]{2,1,0:T(8,128)(2,1)S(1)}, bf16[4,168,128]{2,1,0:T(8,128)(2,1)S(1)}, u32[]{:S(2)}, u32[]{:S(2)}) collective-permute-start(bf16[4,168,128]{2,1,0:T(8,128)(2,1)S(1)} %get-tuple-element.28), channel_id=1, source_target_pairs={{0,6},{1,7},{2,4},{3,5},{4,2},{5,3},{6,0},{7,1},{8,14},{9,15},{10,... | collective-permute-start | bytes 516104 | tf_op jit(solution)/shard_map/ppermute | solution.py:221
  30.7 0.0 collective-permute-done.7.refs_1_
  30.7 0.0 collective-permute-done.8.refs_3_
  30.7 0.0 copy-start
  30.7 1.6 %copy-done = bf16[64,128,128]{2,1,0:T(8,128)(2,1)S(1)} copy-done((bf16[64,128,128]{2,1,0:T(8,128)(2,1)S(1)}, bf16[64,128,128]{2,1,0:T(8,128)(2,1)}, u32[]{:S(2)}) %copy-start) | copy-done | bytes 2097176
  32.3 0.0 copy-start.2
  32.3 1.1 %copy-done.2 = f32[168,1024]{1,0:T(8,128)S(1)} copy-done((f32[168,1024]{1,0:T(8,128)S(1)}, f32[168,1024]{1,0:T(8,128)}, u32[]{:S(2)}) %copy-start.2) | copy-done | bytes 688152
  33.4 0.0 copy-start.1
  33.4 2.7 %reflect.3.total_ref = f32[168,1024]{1,0:T(8,128)S(1)} custom-call(s32[3,73]{1,0:T(4,128)S(1)} %plan.1.order_ref, f32[168,1024]{1,0:T(8,128)S(1)} %copy-done.2, bf16[64,128,128]{2,1,0:T(8,128)(2,1)S(1)} %copy-done, bf16[8,168,128]{2,1,0:T(8,128)(2,1)S(1)} %get-tuple-element.19.refs_0_, bf16[8,168,128]{2,1,0:T(8,128)(2,1)S(1)} %collective-permute-done.7.refs_1_, ...), custom_call_target="tpu_custom_call" | custom-call | tf_op jit(solution)/shard_map/reflect/pallas_call | solution.py:196
  36.1 0.0 collective-permute-done.9.refs_4_
  36.1 0.0 copy-done.1
  36.1 2.1 %reflect.4.total_ref = f32[168,1024]{1,0:T(8,128)S(1)} custom-call(s32[3,73]{1,0:T(4,128)S(1)} %plan.1.order_ref, f32[168,1024]{1,0:T(8,128)S(1)} %reflect.3.total_ref, bf16[64,128,128]{2,1,0:T(8,128)(2,1)S(1)} %copy-done.1, bf16[8,168,128]{2,1,0:T(8,128)(2,1)S(1)} %collective-permute-done.3.refs_0_, ...), custom_call_target="tpu_custom_call" | custom-call | tf_op jit(solution)/shard_map/reflect/pallas_call | solution.py:196
  38.2 2.1 %collective-permute-done.11.refs_1_ = bf16[4,168,128]{2,1,0:T(8,128)(2,1)S(1)} collective-permute-done((bf16[4,168,128]{2,1,0:T(8,128)(2,1)S(1)}, bf16[4,168,128]{2,1,0:T(8,128)(2,1)S(1)}, u32[]{:S(2)}, u32[]{:S(2)}) %collective-permute-start.11) | collective-permute-done | bytes 172064 | tf_op jit(solution)/shard_map/ppermute | solution.py:221
  40.3 0.0 collective-permute-done.10.refs_0_
  40.3 2.2 %reflect.5 = f32[168,1024]{1,0:T(8,128)} custom-call(s32[3,73]{1,0:T(4,128)S(1)} %plan.1.order_ref, f32[168,1024]{1,0:T(8,128)S(1)} %reflect.4.total_ref, bf16[64,128,128]{2,1,0:T(8,128)(2,1)S(1)} %copy-done.1, bf16[6,168,128]{2,1,0:T(8,128)(2,1)S(1)} %collective-permute-done.10.refs_0_, bf16[4,168,128]{2,1,0:T(8,128)(2,1)S(1)} %collective-permute-done.11.refs_1_), custom_call_target="tpu_custom_call" | custom-call | tf_op jit(solution)/shard_map/reflect/pallas_call | solution.py:196
  (2 shorter events, 0.0 us)
Async XLA Ops:
  0.0 10.8 %copy-start.6 = (s32[64]{0:T(128)S(1)}, s32[64]{0:T(128)}, u32[]{:S(2)}) copy-start(s32[64]{0:T(128)} %cols_ref.1) | copy-start | bytes 772
  0.0 19.6 %copy-start.5 = (s32[64]{0:T(128)S(1)}, s32[64]{0:T(128)}, u32[]{:S(2)}) copy-start(s32[64]{0:T(128)} %rows_ref.1) | copy-start | bytes 772
  0.0 19.6 %copy-start.7 = (s32[16]{0:T(128)S(1)}, s32[16]{0:T(128)}, u32[]{:S(2)}) copy-start(s32[16]{0:T(128)} %constant.14.clone.local_ref) | copy-start | bytes 196
  0.0 19.7 %copy-start.8 = (s32[16]{0:T(128)S(1)}, s32[16]{0:T(128)}, u32[]{:S(2)}) copy-start(s32[16]{0:T(128)} %constant.13.clone.base_ref) | copy-start | bytes 196
  0.0 19.7 %copy-start.9 = (s32[16]{0:T(128)S(1)}, s32[16]{0:T(128)}, u32[]{:S(2)}) copy-start(s32[16]{0:T(128)} %constant.12.clone.phase_ref) | copy-start | bytes 196
  3.9 20.3 %collective-permute-start.3 = (bf16[8,168,128]{2,1,0:T(8,128)(2,1)S(1)}, bf16[8,168,128]{2,1,0:T(8,128)(2,1)S(1)}, u32[]{:S(2)}, u32[]{:S(2)}) collective-permute-start(bf16[8,168,128]{2,1,0:T(8,128)(2,1)S(1)} %get-tuple-element.19.refs_0_), channel_id=1, source_target_pairs={{0,8},{1,9},{2,10},{3,11},{4,12},{5,13},{6,14},{7,15},{8,0},{9,1},... | collective-permute-start | bytes 1032200 | tf_op jit(solution)/shard_map/ppermute | solution.py:221
  8.0 16.2 %collective-permute-start.2 = (bf16[8,168,128]{2,1,0:T(8,128)(2,1)S(1)}, bf16[8,168,128]{2,1,0:T(8,128)(2,1)S(1)}, u32[]{:S(2)}, u32[]{:S(2)}) collective-permute-start(bf16[8,168,128]{2,1,0:T(8,128)(2,1)S(1)} %get-tuple-element.19.refs_0_), channel_id=1, source_target_pairs={{0,4},{1,5},{2,6},{3,7},{4,0},{5,1},{6,2},{7,3},{8,12},{9,13},{10,... | collective-permute-start | bytes 1032200 | tf_op jit(solution)/shard_map/ppermute | solution.py:221
  11.0 4.1 %copy-start.3 = (s32[1,128]{1,0:T(1,128)}, s32[1,128]{1,0:T(1,128)S(1)}, u32[]{:S(2)}) copy-start(s32[1,128]{1,0:T(1,128)S(1)} %reads.1.after_ref.reads_ref) | copy-start | bytes 1540
  11.0 3.6 %collective-permute-start = (s32[1,128]{1,0:T(1,128)S(1)}, s32[1,128]{1,0:T(1,128)S(1)}, u32[]{:S(2)}, u32[]{:S(2)}) collective-permute-start(s32[1,128]{1,0:T(1,128)S(1)} %reads.1.after_ref.reads_ref), channel_id=1, source_target_pairs={{0,2},{1,3},{2,0},{3,1},{4,6},{5,7},{6,4},{7,5},{8,10},{9,11},{10,... | collective-permute-start | bytes 1544 | tf_op jit(solution)/shard_map/ppermute | solution.py:221
  12.6 12.3 %collective-permute-start.6 = (bf16[8,168,128]{2,1,0:T(8,128)(2,1)S(1)}, bf16[8,168,128]{2,1,0:T(8,128)(2,1)S(1)}, u32[]{:S(2)}, u32[]{:S(2)}) collective-permute-start(bf16[8,168,128]{2,1,0:T(8,128)(2,1)S(1)} %get-tuple-element.19.refs_0_), channel_id=1, source_target_pairs={{0,2},{1,3},{2,0},{3,1},{4,6},{5,7},{6,4},{7,5},{8,10},{9,11},{10,... | collective-permute-start | bytes 1032200 | tf_op jit(solution)/shard_map/ppermute | solution.py:221
  14.7 9.6 %collective-permute-start.1 = (s32[2,128]{1,0:T(2,128)S(1)}, s32[2,128]{1,0:T(2,128)S(1)}, u32[]{:S(2)}, u32[]{:S(2)}) collective-permute-start(s32[2,128]{1,0:T(2,128)S(1)} %pad_add_fusion.1), channel_id=1, source_target_pairs={{0,4},{1,5},{2,6},{3,7},{4,0},{5,1},{6,2},{7,3},{8,12},{9,13},{10,... | collective-permute-start | bytes 3080 | tf_op jit(solution)/shard_map/ppermute | solution.py:221
  19.7 0.6 %copy-start.4 = (s32[1,128]{1,0:T(1,128)S(1)}, s32[1,128]{1,0:T(1,128)}, u32[]{:S(2)}) copy-start(s32[1,128]{1,0:T(1,128)} %copy-done.3) | copy-start | bytes 1540
  20.3 0.7 %copy-start.10 = (s32[1,128]{1,0:T(1,128)S(1)}, s32[1,128]{1,0:T(1,128)}, u32[]{:S(2)}) copy-start(s32[1,128]{1,0:T(1,128)} %get-tuple-element.18.refs_0_) | copy-start | bytes 1540
  24.3 1.7 %collective-permute-start.5 = (bf16[8,168,128]{2,1,0:T(8,128)(2,1)S(1)}, bf16[8,168,128]{2,1,0:T(8,128)(2,1)S(1)}, u32[]{:S(2)}, u32[]{:S(2)}) collective-permute-start(bf16[8,168,128]{2,1,0:T(8,128)(2,1)S(1)} %collective-permute-done.2.refs_2_), channel_id=1, source_target_pairs={{0,1},{1,0},{2,3},{3,2},{4,5},{5,4},{6,7},{7,6},{8,9},{9,8},{10,11... | collective-permute-start | bytes 1032200 | tf_op jit(solution)/shard_map/ppermute | solution.py:221
  24.4 2.1 %collective-permute-start.4 = (bf16[8,168,128]{2,1,0:T(8,128)(2,1)S(1)}, bf16[8,168,128]{2,1,0:T(8,128)(2,1)S(1)}, u32[]{:S(2)}, u32[]{:S(2)}) collective-permute-start(bf16[8,168,128]{2,1,0:T(8,128)(2,1)S(1)} %collective-permute-done.3.refs_0_), channel_id=1, source_target_pairs={{0,1},{1,0},{2,3},{3,2},{4,5},{5,4},{6,7},{7,6},{8,9},{9,8},{10,11... | collective-permute-start | bytes 1032200 | tf_op jit(solution)/shard_map/ppermute | solution.py:221
  24.9 5.8 %collective-permute-start.7 = (bf16[8,168,128]{2,1,0:T(8,128)(2,1)S(1)}, bf16[8,168,128]{2,1,0:T(8,128)(2,1)S(1)}, u32[]{:S(2)}, u32[]{:S(2)}) collective-permute-start(bf16[8,168,128]{2,1,0:T(8,128)(2,1)S(1)} %get-tuple-element.19.refs_0_), channel_id=1, source_target_pairs={{0,1},{1,0},{2,3},{3,2},{4,5},{5,4},{6,7},{7,6},{8,9},{9,8},{10,11... | collective-permute-start | bytes 1032200 | tf_op jit(solution)/shard_map/ppermute | solution.py:221
  24.9 5.7 %collective-permute-start.8 = (bf16[8,168,128]{2,1,0:T(8,128)(2,1)S(1)}, bf16[8,168,128]{2,1,0:T(8,128)(2,1)S(1)}, u32[]{:S(2)}, u32[]{:S(2)}) collective-permute-start(bf16[8,168,128]{2,1,0:T(8,128)(2,1)S(1)} %collective-permute-done.6.refs_3_.refs_2_), channel_id=1, source_target_pairs={{0,1},{1,0},{2,3},{3,2},{4,5},{5,4},{6,7},{7,6},{8,9},{9,8},{10,11... | collective-permute-start | bytes 1032200 | tf_op jit(solution)/shard_map/ppermute | solution.py:221
  27.1 9.0 %collective-permute-start.9 = (bf16[6,168,128]{2,1,0:T(8,128)(2,1)S(1)}, bf16[6,168,128]{2,1,0:T(8,128)(2,1)S(1)}, u32[]{:S(2)}, u32[]{:S(2)}) collective-permute-start(bf16[6,168,128]{2,1,0:T(8,128)(2,1)S(1)} %get-tuple-element.25), channel_id=1, source_target_pairs={{0,2},{1,3},{2,0},{3,1},{4,6},{5,7},{6,4},{7,5},{8,10},{9,11},{10,... | collective-permute-start | bytes 774152 | tf_op jit(solution)/shard_map/ppermute | solution.py:221
  28.2 12.1 %collective-permute-start.10 = (bf16[6,168,128]{2,1,0:T(8,128)(2,1)S(1)}, bf16[6,168,128]{2,1,0:T(8,128)(2,1)S(1)}, u32[]{:S(2)}, u32[]{:S(2)}) collective-permute-start(bf16[6,168,128]{2,1,0:T(8,128)(2,1)S(1)} %get-tuple-element.27), channel_id=1, source_target_pairs={{0,4},{1,5},{2,6},{3,7},{4,0},{5,1},{6,2},{7,3},{8,12},{9,13},{10,... | collective-permute-start | bytes 774152 | tf_op jit(solution)/shard_map/ppermute | solution.py:221
  29.7 10.6 %collective-permute-start.11 = (bf16[4,168,128]{2,1,0:T(8,128)(2,1)S(1)}, bf16[4,168,128]{2,1,0:T(8,128)(2,1)S(1)}, u32[]{:S(2)}, u32[]{:S(2)}) collective-permute-start(bf16[4,168,128]{2,1,0:T(8,128)(2,1)S(1)} %get-tuple-element.28), channel_id=1, source_target_pairs={{0,6},{1,7},{2,4},{3,5},{4,2},{5,3},{6,0},{7,1},{8,14},{9,15},{10,... | collective-permute-start | bytes 516104 | tf_op jit(solution)/shard_map/ppermute | solution.py:221
  30.7 1.6 %copy-start = (bf16[64,128,128]{2,1,0:T(8,128)(2,1)S(1)}, bf16[64,128,128]{2,1,0:T(8,128)(2,1)}, u32[]{:S(2)}) copy-start(bf16[64,128,128]{2,1,0:T(8,128)(2,1)} %views_ref.5) | copy-start | bytes 6291460
  32.3 1.1 %copy-start.2 = (f32[168,1024]{1,0:T(8,128)S(1)}, f32[168,1024]{1,0:T(8,128)}, u32[]{:S(2)}) copy-start(f32[168,1024]{1,0:T(8,128)} %get-tuple-element.26.total_ref) | copy-start | bytes 2064388
  33.4 2.7 %copy-start.1 = (bf16[64,128,128]{2,1,0:T(8,128)(2,1)S(1)}, bf16[64,128,128]{2,1,0:T(8,128)(2,1)}, u32[]{:S(2)}) copy-start(bf16[64,128,128]{2,1,0:T(8,128)(2,1)} %views_ref.5) | copy-start | bytes 6291460
where the time goes:
time: 42.4 us; the launch traced here: 42.5 us
  Pallas kernels  19.5 us (46%)
  starting transfers between devices  12.8 us (30%)
  waiting for transfers between devices  4.12 us (10%)
  local copies, waits for them, and re-layouts  3.98 us (9%)
  between operations  1.41 us (3%)
  other arithmetic  0.63 us (1%)
    ppermute x12, starting transfers between devices, swap(): return lax.ppermute(x, 'tiles', [(i, i ^ bits) for i in range(peers)])  12.8 us
    pallas_call x2, Pallas kernels, product(): pl.pallas_call(functools.partial(product_kernel, cuts), in_specs=[ANY, HB...  8.43 us
    pallas_call x3, Pallas kernels, reflect(): pl.pallas_call(functools.partial(reflect_kernel, phase), in_specs=[HBM, H...  7.03 us
    ppermute x12, waiting for transfers between devices, swap(): return lax.ppermute(x, 'tiles', [(i, i ^ bits) for i in range(peers)])  4.12 us
    unnamed x22, local copies, waits for them, and re-layouts  3.98 us
    pallas_call x1, Pallas kernels, plan(): pl.pallas_call(functools.partial(plan_kernel, blocks, rooms, phase.shape[...  3.29 us
  transfers between devices with their start and end apart: 12, of which 3 were waited for; matrix products, arithmetic and copies ran while one was open for 1% of the time, Pallas kernels for 32%

commit v1 on v0

--- a/solution.py
+++ b/solution.py
@@ -123,16 +123,16 @@
 
     def step(slot, carry):
         col = cols_ref[slot]
-        group = col // blocks
+        group = col >> (blocks.bit_length() - 1)
         kind = group ^ me_ref[0]
-        inside = col - group * blocks
+        inside = col & (blocks - 1)
         local = local_ref[kind] == 1
         end = (inside == reads_ref[0, groups + group]).astype(jnp.int32)
         source = base_ref[kind] + jnp.where(local, inside, end)
-        row = rows_ref[slot] - me_ref[0] * blocks
+        row = rows_ref[slot] & (blocks - 1)
         phase = phase_ref[kind]
         at = order_ref[phase, 0] + 1
-        order_ref[phase, at] = slot + row * 256 + source * 4096
+        order_ref[phase, at] = slot | (row << 8) | (source << 12)
         order_ref[phase, 0] = at
         return carry
 
@@ -176,7 +176,7 @@
         entries = [order[phase, 1 + i * AT_ONCE + k] for k in range(AT_ONCE)]
         parts = [
             lax.dot_general(
-                pool[entry // 4096],
+                pool[entry >> 12],
                 views_ref[entry & 255],
                 (((1,), (1,)), ((), ())),
                 preferred_element_type=jnp.float32,
@@ -184,7 +184,7 @@
             for entry in entries
         ]
         for entry, part in zip(entries, parts):
-            columns = pl.ds(pl.multiple_of(((entry // 256) & 15) * block, block), block)
+            columns = pl.ds(pl.multiple_of(((entry >> 8) & 15) * block, block), block)
             out_ref[:, columns] += part
         return carry
 

time: 42.4 us -> 42.3 us (level); the launches traced: 42.5 us -> 41.8 us
  Pallas kernels: 19.5 us -> 15.6 us
  waiting for transfers between devices: 4.12 us -> 7.42 us
    ppermute x12, waiting for transfers between devices: 4.12 us -> 7.42 us  [swap(): return lax.ppermute(x, 'tiles', [(i, i ^ bits) for i in range(peers)])]
    pallas_call x3, Pallas kernels: 7.03 us -> 4.39 us  [reflect(): pl.pallas_call(functools.partial(reflect_kernel, phase), in_specs=[HBM, H...]
    pallas_call x1, Pallas kernels: 3.29 us -> 1.98 us  [plan(): pl.pallas_call(functools.partial(plan_kernel, blocks, rooms, phase.shape[...]
  transfers between devices with their start and end apart: 12 -> 12, of which waited for: 3 -> 5; matrix products, arithmetic and copies ran while one was open for 1% -> 1% of each run, Pallas kernels for 32% -> 24%
where the time goes in v1:
time: 42.3 us; the launch traced here: 41.8 us
  Pallas kernels  15.6 us (37%)
  starting transfers between devices  12.8 us (30%)
  waiting for transfers between devices  7.42 us (18%)
  local copies, waits for them, and re-layouts  3.98 us (9%)
  between operations  1.37 us (3%)
  other arithmetic  0.63 us (1%)
    ppermute x12, starting transfers between devices, swap(): return lax.ppermute(x, 'tiles', [(i, i ^ bits) for i in range(peers)])  12.8 us
    pallas_call x2, Pallas kernels, product(): pl.pallas_call(functools.partial(product_kernel, cuts), in_specs=[ANY, HB...  8.43 us
    ppermute x12, waiting for transfers between devices, swap(): return lax.ppermute(x, 'tiles', [(i, i ^ bits) for i in range(peers)])  7.42 us
    pallas_call x3, Pallas kernels, reflect(): pl.pallas_call(functools.partial(reflect_kernel, phase), in_specs=[HBM, H...  4.39 us
    unnamed x22, local copies, waits for them, and re-layouts  3.98 us
    pallas_call x1, Pallas kernels, plan(): pl.pallas_call(functools.partial(plan_kernel, blocks, rooms, phase.shape[...  1.98 us
  transfers between devices with their start and end apart: 12, of which 5 were waited for; matrix products, arithmetic and copies ran while one was open for 1% of the time, Pallas kernels for 24%

profile of v1, /device:TPU:0, one launch (start us, length us, event | category | flops | bytes accessed | tf_op | source)
XLA Modules:
  0.0 41.8 jit_solution(16778586748646457547)
XLA Ops:
  0.0 0.0 copy-start.6
  0.0 0.0 copy-start.5
  0.0 0.0 copy-start.7
  0.0 0.0 copy-start.8
  0.0 0.0 copy-start.9
  0.0 3.9 %emitted.1 = (bf16[8,168,128]{2,1,0:T(8,128)(2,1)S(1)}, s32[1,128]{1,0:T(1,128)}) custom-call(s32[1]{0:T(128)} %bitcast.after_ref.me_ref, bf16[168,2306]{1,0:T(8,128)(2,1)} %sky_ref.3, bf16[2306,1024]{1,0:T(8,128)(2,1)} %coeffs_ref.3, f32[1,1024]{1,0:T(1,128)} %bitcast.8), custom_call_target="tpu_custom_call" | custom-call | tf_op jit(solution)/shard_map/emitted/pallas_call | solution.py:51
  3.9 4.1 %collective-permute-start.3 = (bf16[8,168,128]{2,1,0:T(8,128)(2,1)S(1)}, bf16[8,168,128]{2,1,0:T(8,128)(2,1)S(1)}, u32[]{:S(2)}, u32[]{:S(2)}) collective-permute-start(bf16[8,168,128]{2,1,0:T(8,128)(2,1)S(1)} %get-tuple-element.19.refs_0_), channel_id=1, source_target_pairs={{0,8},{1,9},{2,10},{3,11},{4,12},{5,13},{6,14},{7,15},{8,0},{9,1},... | collective-permute-start | bytes 1032200 | tf_op jit(solution)/shard_map/ppermute | solution.py:221
  8.0 1.6 %collective-permute-start.2 = (bf16[8,168,128]{2,1,0:T(8,128)(2,1)S(1)}, bf16[8,168,128]{2,1,0:T(8,128)(2,1)S(1)}, u32[]{:S(2)}, u32[]{:S(2)}) collective-permute-start(bf16[8,168,128]{2,1,0:T(8,128)(2,1)S(1)} %get-tuple-element.19.refs_0_), channel_id=1, source_target_pairs={{0,4},{1,5},{2,6},{3,7},{4,0},{5,1},{6,2},{7,3},{8,12},{9,13},{10,... | collective-permute-start | bytes 1032200 | tf_op jit(solution)/shard_map/ppermute | solution.py:221
  10.8 0.0 copy-done.6
  10.8 0.2 reads.1.after_ref.reads_ref
  11.0 0.0 copy-start.3
  11.0 1.6 %collective-permute-start = (s32[1,128]{1,0:T(1,128)S(1)}, s32[1,128]{1,0:T(1,128)S(1)}, u32[]{:S(2)}, u32[]{:S(2)}) collective-permute-start(s32[1,128]{1,0:T(1,128)S(1)} %reads.1.after_ref.reads_ref), channel_id=1, source_target_pairs={{0,2},{1,3},{2,0},{3,1},{4,6},{5,7},{6,4},{7,5},{8,10},{9,11},{10,... | collective-permute-start | bytes 1544 | tf_op jit(solution)/shard_map/ppermute | solution.py:221
  12.6 0.5 %collective-permute-start.6 = (bf16[8,168,128]{2,1,0:T(8,128)(2,1)S(1)}, bf16[8,168,128]{2,1,0:T(8,128)(2,1)S(1)}, u32[]{:S(2)}, u32[]{:S(2)}) collective-permute-start(bf16[8,168,128]{2,1,0:T(8,128)(2,1)S(1)} %get-tuple-element.19.refs_0_), channel_id=1, source_target_pairs={{0,2},{1,3},{2,0},{3,1},{4,6},{5,7},{6,4},{7,5},{8,10},{9,11},{10,... | collective-permute-start | bytes 1032200 | tf_op jit(solution)/shard_map/ppermute | solution.py:221
  13.1 1.5 %collective-permute-done = s32[1,128]{1,0:T(1,128)S(1)} collective-permute-done((s32[1,128]{1,0:T(1,128)S(1)}, s32[1,128]{1,0:T(1,128)S(1)}, u32[]{:S(2)}, u32[]{:S(2)}) %collective-permute-start) | collective-permute-done | bytes 544 | tf_op jit(solution)/shard_map/ppermute | solution.py:221
  14.7 0.4 %collective-permute-start.1 = (s32[2,128]{1,0:T(2,128)S(1)}, s32[2,128]{1,0:T(2,128)S(1)}, u32[]{:S(2)}, u32[]{:S(2)}) collective-permute-start(s32[2,128]{1,0:T(2,128)S(1)} %pad_add_fusion.1), channel_id=1, source_target_pairs={{0,4},{1,5},{2,6},{3,7},{4,0},{5,1},{6,2},{7,3},{8,12},{9,13},{10,... | collective-permute-start | bytes 3080 | tf_op jit(solution)/shard_map/ppermute | solution.py:221
  15.1 0.0 copy-done.3
  15.1 4.5 %direct.1 = (f32[168,1024]{1,0:T(8,128)}, s32[1,128]{1,0:T(1,128)}) custom-call(s32[1,128]{1,0:T(1,128)} %copy-done.3, bf16[168,2306]{1,0:T(8,128)(2,1)} %sky_ref.3, bf16[2306,1024]{1,0:T(8,128)(2,1)} %coeffs_ref.3, f32[1,1024]{1,0:T(1,128)} %bitcast.9), custom_call_target="tpu_custom_call" | custom-call | tf_op jit(solution)/shard_map/direct/pallas_call | solution.py:51
  19.6 0.0 copy-done.5
  19.6 0.0 copy-done.7
  19.7 0.0 copy-done.8
  19.7 0.0 copy-done.9
  19.7 0.0 copy-start.4
  19.7 0.6 %copy-done.4 = s32[1,128]{1,0:T(1,128)S(1)} copy-done((s32[1,128]{1,0:T(1,128)S(1)}, s32[1,128]{1,0:T(1,128)}, u32[]{:S(2)}) %copy-start.4) | copy-done | bytes 536
  20.3 0.0 copy-start.10
  20.3 0.7 %copy-done.10 = s32[1,128]{1,0:T(1,128)S(1)} copy-done((s32[1,128]{1,0:T(1,128)S(1)}, s32[1,128]{1,0:T(1,128)}, u32[]{:S(2)}) %copy-start.10) | copy-done | bytes 536
  20.9 2.0 %plan.1.order_ref = s32[3,73]{1,0:T(4,128)S(1)} custom-call(s32[1]{0:T(128)} %bitcast.after_ref.me_ref, s32[64]{0:T(128)S(1)} %copy-done.5, s32[64]{0:T(128)S(1)} %copy-done.6, s32[1,128]{1,0:T(1,128)S(1)} %copy-done.4, s32[16]{0:T(128)S(1)} %copy-done.9, s32[16]{0:T(128)S(1)} %copy-done.8, s32[16]{0:T(128)S(1)} %copy-done.7, s32[1,128]{1,0:T(1,128)S(1)} %copy-done.10), custom_call_target="tpu_custom_call" | custom-call | tf_op jit(solution)/shard_map/plan/pallas_call | solution.py:143
  22.9 0.9 %collective-permute-done.1 = s32[2,128]{1,0:T(2,128)S(1)} collective-permute-done((s32[2,128]{1,0:T(2,128)S(1)}, s32[2,128]{1,0:T(2,128)S(1)}, u32[]{:S(2)}, u32[]{:S(2)}) %collective-permute-start.1) | collective-permute-done | bytes 1056 | tf_op jit(solution)/shard_map/ppermute | solution.py:221
  23.8 0.0 collective-permute-done.3.refs_0_
  23.8 0.0 collective-permute-done.2.refs_2_
  23.8 0.0 collective-permute-start.5
  23.8 0.5 %collective-permute-start.4 = (bf16[8,168,128]{2,1,0:T(8,128)(2,1)S(1)}, bf16[8,168,128]{2,1,0:T(8,128)(2,1)S(1)}, u32[]{:S(2)}, u32[]{:S(2)}) collective-permute-start(bf16[8,168,128]{2,1,0:T(8,128)(2,1)S(1)} %collective-permute-done.3.refs_0_), channel_id=1, source_target_pairs={{0,1},{1,0},{2,3},{3,2},{4,5},{5,4},{6,7},{7,6},{8,9},{9,8},{10,11... | collective-permute-start | bytes 1032200 | tf_op jit(solution)/shard_map/ppermute | solution.py:221
  24.3 0.1 collective-permute-start.7
  24.4 0.0 collective-permute-done.6.refs_3_.refs_2_
  24.4 0.4 %collective-permute-start.8 = (bf16[8,168,128]{2,1,0:T(8,128)(2,1)S(1)}, bf16[8,168,128]{2,1,0:T(8,128)(2,1)S(1)}, u32[]{:S(2)}, u32[]{:S(2)}) collective-permute-start(bf16[8,168,128]{2,1,0:T(8,128)(2,1)S(1)} %collective-permute-done.6.refs_3_.refs_2_), channel_id=1, source_target_pairs={{0,1},{1,0},{2,3},{3,2},{4,5},{5,4},{6,7},{7,6},{8,9},{9,8},{10,11... | collective-permute-start | bytes 1032200 | tf_op jit(solution)/shard_map/ppermute | solution.py:221
  24.9 0.6 %pad_add_fusion.table_ref = s32[4,128]{1,0:T(4,128)S(1)} fusion(s32[2,128]{1,0:T(2,128)S(1)} %collective-permute-done.1, s32[1,128]{1,0:T(1,128)S(1)} %collective-permute-done, s32[1,128]{1,0:T(1,128)} %copy-done.3), kind=kLoop, calls=%fused_computation | loop fusion | flops 1024 | bytes 4096 | tf_op jit(solution)/shard_map/concatenate | solution.py:268
  25.5 0.0 collective-permute-done.5.refs_2_.refs_3_
  25.5 0.5 %collective-permute-done.4.refs_1_ = bf16[8,168,128]{2,1,0:T(8,128)(2,1)S(1)} collective-permute-done((bf16[8,168,128]{2,1,0:T(8,128)(2,1)S(1)}, bf16[8,168,128]{2,1,0:T(8,128)(2,1)S(1)}, u32[]{:S(2)}, u32[]{:S(2)}) %collective-permute-start.4) | collective-permute-done | bytes 344096 | tf_op jit(solution)/shard_map/ppermute | solution.py:221
  26.0 0.6 %pack.1 = (bf16[6,168,128]{2,1,0:T(8,128)(2,1)S(1)}, bf16[6,168,128]{2,1,0:T(8,128)(2,1)S(1)}, bf16[4,168,128]{2,1,0:T(8,128)(2,1)S(1)}) custom-call(s32[1]{0:T(128)} %bitcast.after_ref.me_ref, s32[4,128]{1,0:T(4,128)S(1)} %pad_add_fusion.table_ref, bf16[8,168,128]{2,1,0:T(8,128)(2,1)S(1)} %collective-permute-done.3.refs_0_, ...), custom_call_target="tpu_custom_call" | custom-call | tf_op jit(solution)/shard_map/pack/pallas_call | solution.py:101
  26.6 1.9 %collective-permute-start.9 = (bf16[6,168,128]{2,1,0:T(8,128)(2,1)S(1)}, bf16[6,168,128]{2,1,0:T(8,128)(2,1)S(1)}, u32[]{:S(2)}, u32[]{:S(2)}) collective-permute-start(bf16[6,168,128]{2,1,0:T(8,128)(2,1)S(1)} %get-tuple-element.25), channel_id=1, source_target_pairs={{0,2},{1,3},{2,0},{3,1},{4,6},{5,7},{6,4},{7,5},{8,10},{9,11},{10,... | collective-permute-start | bytes 774152 | tf_op jit(solution)/shard_map/ppermute | solution.py:221
  28.5 1.6 %collective-permute-start.10 = (bf16[6,168,128]{2,1,0:T(8,128)(2,1)S(1)}, bf16[6,168,128]{2,1,0:T(8,128)(2,1)S(1)}, u32[]{:S(2)}, u32[]{:S(2)}) collective-permute-start(bf16[6,168,128]{2,1,0:T(8,128)(2,1)S(1)} %get-tuple-element.27), channel_id=1, source_target_pairs={{0,4},{1,5},{2,6},{3,7},{4,0},{5,1},{6,2},{7,3},{8,12},{9,13},{10,... | collective-permute-start | bytes 774152 | tf_op jit(solution)/shard_map/ppermute | solution.py:221
  30.0 0.1 collective-permute-start.11
  30.2 0.0 collective-permute-done.7.refs_1_
  30.2 0.0 collective-permute-done.8.refs_3_
  30.2 0.0 copy-start
  30.2 1.6 %copy-done = bf16[64,128,128]{2,1,0:T(8,128)(2,1)S(1)} copy-done((bf16[64,128,128]{2,1,0:T(8,128)(2,1)S(1)}, bf16[64,128,128]{2,1,0:T(8,128)(2,1)}, u32[]{:S(2)}) %copy-start) | copy-done | bytes 2097176
  31.8 0.0 copy-start.2
  31.8 1.1 %copy-done.2 = f32[168,1024]{1,0:T(8,128)S(1)} copy-done((f32[168,1024]{1,0:T(8,128)S(1)}, f32[168,1024]{1,0:T(8,128)}, u32[]{:S(2)}) %copy-start.2) | copy-done | bytes 688152
  32.9 0.0 copy-start.1
  32.9 1.2 %reflect.3.total_ref = f32[168,1024]{1,0:T(8,128)S(1)} custom-call(s32[3,73]{1,0:T(4,128)S(1)} %plan.1.order_ref, f32[168,1024]{1,0:T(8,128)S(1)} %copy-done.2, bf16[64,128,128]{2,1,0:T(8,128)(2,1)S(1)} %copy-done, bf16[8,168,128]{2,1,0:T(8,128)(2,1)S(1)} %get-tuple-element.19.refs_0_, bf16[8,168,128]{2,1,0:T(8,128)(2,1)S(1)} %collective-permute-done.7.refs_1_, ...), custom_call_target="tpu_custom_call" | custom-call | tf_op jit(solution)/shard_map/reflect/pallas_call | solution.py:196
  34.1 0.9 %collective-permute-done.9.refs_4_ = bf16[6,168,128]{2,1,0:T(8,128)(2,1)S(1)} collective-permute-done((bf16[6,168,128]{2,1,0:T(8,128)(2,1)S(1)}, bf16[6,168,128]{2,1,0:T(8,128)(2,1)S(1)}, u32[]{:S(2)}, u32[]{:S(2)}) %collective-permute-start.9) | collective-permute-done | bytes 258080 | tf_op jit(solution)/shard_map/ppermute | solution.py:221
  35.0 0.0 copy-done.1
  35.0 1.3 %reflect.4.total_ref = f32[168,1024]{1,0:T(8,128)S(1)} custom-call(s32[3,73]{1,0:T(4,128)S(1)} %plan.1.order_ref, f32[168,1024]{1,0:T(8,128)S(1)} %reflect.3.total_ref, bf16[64,128,128]{2,1,0:T(8,128)(2,1)S(1)} %copy-done.1, bf16[8,168,128]{2,1,0:T(8,128)(2,1)S(1)} %collective-permute-done.3.refs_0_, ...), custom_call_target="tpu_custom_call" | custom-call | tf_op jit(solution)/shard_map/reflect/pallas_call | solution.py:196
  36.3 3.6 %collective-permute-done.11.refs_1_ = bf16[4,168,128]{2,1,0:T(8,128)(2,1)S(1)} collective-permute-done((bf16[4,168,128]{2,1,0:T(8,128)(2,1)S(1)}, bf16[4,168,128]{2,1,0:T(8,128)(2,1)S(1)}, u32[]{:S(2)}, u32[]{:S(2)}) %collective-permute-start.11) | collective-permute-done | bytes 172064 | tf_op jit(solution)/shard_map/ppermute | solution.py:221
  39.9 0.0 collective-permute-done.10.refs_0_
  39.9 1.8 %reflect.5 = f32[168,1024]{1,0:T(8,128)} custom-call(s32[3,73]{1,0:T(4,128)S(1)} %plan.1.order_ref, f32[168,1024]{1,0:T(8,128)S(1)} %reflect.4.total_ref, bf16[64,128,128]{2,1,0:T(8,128)(2,1)S(1)} %copy-done.1, bf16[6,168,128]{2,1,0:T(8,128)(2,1)S(1)} %collective-permute-done.10.refs_0_, bf16[4,168,128]{2,1,0:T(8,128)(2,1)S(1)} %collective-permute-done.11.refs_1_), custom_call_target="tpu_custom_call" | custom-call | tf_op jit(solution)/shard_map/reflect/pallas_call | solution.py:196
  (2 shorter events, 0.0 us)
Async XLA Ops:
  0.0 10.8 %copy-start.6 = (s32[64]{0:T(128)S(1)}, s32[64]{0:T(128)}, u32[]{:S(2)}) copy-start(s32[64]{0:T(128)} %cols_ref.1) | copy-start | bytes 772
  0.0 19.6 %copy-start.5 = (s32[64]{0:T(128)S(1)}, s32[64]{0:T(128)}, u32[]{:S(2)}) copy-start(s32[64]{0:T(128)} %rows_ref.1) | copy-start | bytes 772
  0.0 19.6 %copy-start.7 = (s32[16]{0:T(128)S(1)}, s32[16]{0:T(128)}, u32[]{:S(2)}) copy-start(s32[16]{0:T(128)} %constant.14.clone.local_ref) | copy-start | bytes 196
  0.0 19.7 %copy-start.8 = (s32[16]{0:T(128)S(1)}, s32[16]{0:T(128)}, u32[]{:S(2)}) copy-start(s32[16]{0:T(128)} %constant.13.clone.base_ref) | copy-start | bytes 196
  0.0 19.7 %copy-start.9 = (s32[16]{0:T(128)S(1)}, s32[16]{0:T(128)}, u32[]{:S(2)}) copy-start(s32[16]{0:T(128)} %constant.12.clone.phase_ref) | copy-start | bytes 196
  3.9 19.9 %collective-permute-start.3 = (bf16[8,168,128]{2,1,0:T(8,128)(2,1)S(1)}, bf16[8,168,128]{2,1,0:T(8,128)(2,1)S(1)}, u32[]{:S(2)}, u32[]{:S(2)}) collective-permute-start(bf16[8,168,128]{2,1,0:T(8,128)(2,1)S(1)} %get-tuple-element.19.refs_0_), channel_id=1, source_target_pairs={{0,8},{1,9},{2,10},{3,11},{4,12},{5,13},{6,14},{7,15},{8,0},{9,1},... | collective-permute-start | bytes 1032200 | tf_op jit(solution)/shard_map/ppermute | solution.py:221
  8.0 15.8 %collective-permute-start.2 = (bf16[8,168,128]{2,1,0:T(8,128)(2,1)S(1)}, bf16[8,168,128]{2,1,0:T(8,128)(2,1)S(1)}, u32[]{:S(2)}, u32[]{:S(2)}) collective-permute-start(bf16[8,168,128]{2,1,0:T(8,128)(2,1)S(1)} %get-tuple-element.19.refs_0_), channel_id=1, source_target_pairs={{0,4},{1,5},{2,6},{3,7},{4,0},{5,1},{6,2},{7,3},{8,12},{9,13},{10,... | collective-permute-start | bytes 1032200 | tf_op jit(solution)/shard_map/ppermute | solution.py:221
  11.0 4.1 %copy-start.3 = (s32[1,128]{1,0:T(1,128)}, s32[1,128]{1,0:T(1,128)S(1)}, u32[]{:S(2)}) copy-start(s32[1,128]{1,0:T(1,128)S(1)} %reads.1.after_ref.reads_ref) | copy-start | bytes 1540
  11.0 3.6 %collective-permute-start = (s32[1,128]{1,0:T(1,128)S(1)}, s32[1,128]{1,0:T(1,128)S(1)}, u32[]{:S(2)}, u32[]{:S(2)}) collective-permute-start(s32[1,128]{1,0:T(1,128)S(1)} %reads.1.after_ref.reads_ref), channel_id=1, source_target_pairs={{0,2},{1,3},{2,0},{3,1},{4,6},{5,7},{6,4},{7,5},{8,10},{9,11},{10,... | collective-permute-start | bytes 1544 | tf_op jit(solution)/shard_map/ppermute | solution.py:221
  12.6 11.8 %collective-permute-start.6 = (bf16[8,168,128]{2,1,0:T(8,128)(2,1)S(1)}, bf16[8,168,128]{2,1,0:T(8,128)(2,1)S(1)}, u32[]{:S(2)}, u32[]{:S(2)}) collective-permute-start(bf16[8,168,128]{2,1,0:T(8,128)(2,1)S(1)} %get-tuple-element.19.refs_0_), channel_id=1, source_target_pairs={{0,2},{1,3},{2,0},{3,1},{4,6},{5,7},{6,4},{7,5},{8,10},{9,11},{10,... | collective-permute-start | bytes 1032200 | tf_op jit(solution)/shard_map/ppermute | solution.py:221
  14.7 9.2 %collective-permute-start.1 = (s32[2,128]{1,0:T(2,128)S(1)}, s32[2,128]{1,0:T(2,128)S(1)}, u32[]{:S(2)}, u32[]{:S(2)}) collective-permute-start(s32[2,128]{1,0:T(2,128)S(1)} %pad_add_fusion.1), channel_id=1, source_target_pairs={{0,4},{1,5},{2,6},{3,7},{4,0},{5,1},{6,2},{7,3},{8,12},{9,13},{10,... | collective-permute-start | bytes 3080 | tf_op jit(solution)/shard_map/ppermute | solution.py:221
  19.7 0.6 %copy-start.4 = (s32[1,128]{1,0:T(1,128)S(1)}, s32[1,128]{1,0:T(1,128)}, u32[]{:S(2)}) copy-start(s32[1,128]{1,0:T(1,128)} %copy-done.3) | copy-start | bytes 1540
  20.3 0.7 %copy-start.10 = (s32[1,128]{1,0:T(1,128)S(1)}, s32[1,128]{1,0:T(1,128)}, u32[]{:S(2)}) copy-start(s32[1,128]{1,0:T(1,128)} %get-tuple-element.18.refs_0_) | copy-start | bytes 1540
  23.8 1.7 %collective-permute-start.5 = (bf16[8,168,128]{2,1,0:T(8,128)(2,1)S(1)}, bf16[8,168,128]{2,1,0:T(8,128)(2,1)S(1)}, u32[]{:S(2)}, u32[]{:S(2)}) collective-permute-start(bf16[8,168,128]{2,1,0:T(8,128)(2,1)S(1)} %collective-permute-done.2.refs_2_), channel_id=1, source_target_pairs={{0,1},{1,0},{2,3},{3,2},{4,5},{5,4},{6,7},{7,6},{8,9},{9,8},{10,11... | collective-permute-start | bytes 1032200 | tf_op jit(solution)/shard_map/ppermute | solution.py:221
  23.8 2.1 %collective-permute-start.4 = (bf16[8,168,128]{2,1,0:T(8,128)(2,1)S(1)}, bf16[8,168,128]{2,1,0:T(8,128)(2,1)S(1)}, u32[]{:S(2)}, u32[]{:S(2)}) collective-permute-start(bf16[8,168,128]{2,1,0:T(8,128)(2,1)S(1)} %collective-permute-done.3.refs_0_), channel_id=1, source_target_pairs={{0,1},{1,0},{2,3},{3,2},{4,5},{5,4},{6,7},{7,6},{8,9},{9,8},{10,11... | collective-permute-start | bytes 1032200 | tf_op jit(solution)/shard_map/ppermute | solution.py:221
  24.3 5.8 %collective-permute-start.7 = (bf16[8,168,128]{2,1,0:T(8,128)(2,1)S(1)}, bf16[8,168,128]{2,1,0:T(8,128)(2,1)S(1)}, u32[]{:S(2)}, u32[]{:S(2)}) collective-permute-start(bf16[8,168,128]{2,1,0:T(8,128)(2,1)S(1)} %get-tuple-element.19.refs_0_), channel_id=1, source_target_pairs={{0,1},{1,0},{2,3},{3,2},{4,5},{5,4},{6,7},{7,6},{8,9},{9,8},{10,11... | collective-permute-start | bytes 1032200 | tf_op jit(solution)/shard_map/ppermute | solution.py:221
  24.4 5.7 %collective-permute-start.8 = (bf16[8,168,128]{2,1,0:T(8,128)(2,1)S(1)}, bf16[8,168,128]{2,1,0:T(8,128)(2,1)S(1)}, u32[]{:S(2)}, u32[]{:S(2)}) collective-permute-start(bf16[8,168,128]{2,1,0:T(8,128)(2,1)S(1)} %collective-permute-done.6.refs_3_.refs_2_), channel_id=1, source_target_pairs={{0,1},{1,0},{2,3},{3,2},{4,5},{5,4},{6,7},{7,6},{8,9},{9,8},{10,11... | collective-permute-start | bytes 1032200 | tf_op jit(solution)/shard_map/ppermute | solution.py:221
  26.6 8.4 %collective-permute-start.9 = (bf16[6,168,128]{2,1,0:T(8,128)(2,1)S(1)}, bf16[6,168,128]{2,1,0:T(8,128)(2,1)S(1)}, u32[]{:S(2)}, u32[]{:S(2)}) collective-permute-start(bf16[6,168,128]{2,1,0:T(8,128)(2,1)S(1)} %get-tuple-element.25), channel_id=1, source_target_pairs={{0,2},{1,3},{2,0},{3,1},{4,6},{5,7},{6,4},{7,5},{8,10},{9,11},{10,... | collective-permute-start | bytes 774152 | tf_op jit(solution)/shard_map/ppermute | solution.py:221
  28.5 11.5 %collective-permute-start.10 = (bf16[6,168,128]{2,1,0:T(8,128)(2,1)S(1)}, bf16[6,168,128]{2,1,0:T(8,128)(2,1)S(1)}, u32[]{:S(2)}, u32[]{:S(2)}) collective-permute-start(bf16[6,168,128]{2,1,0:T(8,128)(2,1)S(1)} %get-tuple-element.27), channel_id=1, source_target_pairs={{0,4},{1,5},{2,6},{3,7},{4,0},{5,1},{6,2},{7,3},{8,12},{9,13},{10,... | collective-permute-start | bytes 774152 | tf_op jit(solution)/shard_map/ppermute | solution.py:221
  30.0 9.9 %collective-permute-start.11 = (bf16[4,168,128]{2,1,0:T(8,128)(2,1)S(1)}, bf16[4,168,128]{2,1,0:T(8,128)(2,1)S(1)}, u32[]{:S(2)}, u32[]{:S(2)}) collective-permute-start(bf16[4,168,128]{2,1,0:T(8,128)(2,1)S(1)} %get-tuple-element.28), channel_id=1, source_target_pairs={{0,6},{1,7},{2,4},{3,5},{4,2},{5,3},{6,0},{7,1},{8,14},{9,15},{10,... | collective-permute-start | bytes 516104 | tf_op jit(solution)/shard_map/ppermute | solution.py:221
  30.2 1.6 %copy-start = (bf16[64,128,128]{2,1,0:T(8,128)(2,1)S(1)}, bf16[64,128,128]{2,1,0:T(8,128)(2,1)}, u32[]{:S(2)}) copy-start(bf16[64,128,128]{2,1,0:T(8,128)(2,1)} %views_ref.5) | copy-start | bytes 6291460
  31.8 1.1 %copy-start.2 = (f32[168,1024]{1,0:T(8,128)S(1)}, f32[168,1024]{1,0:T(8,128)}, u32[]{:S(2)}) copy-start(f32[168,1024]{1,0:T(8,128)} %get-tuple-element.26.total_ref) | copy-start | bytes 2064388
  32.9 2.1 %copy-start.1 = (bf16[64,128,128]{2,1,0:T(8,128)(2,1)S(1)}, bf16[64,128,128]{2,1,0:T(8,128)(2,1)}, u32[]{:S(2)}) copy-start(bf16[64,128,128]{2,1,0:T(8,128)(2,1)} %views_ref.5) | copy-start | bytes 6291460
